TPU v7x, 32 devices: a whole 2x2x4 slice. The times are simulated.
32 devices in a mesh: grp: 2 (over x), lon: 16 (over z, y, core).
Axes of the slice: x: 2, y: 2, z: 4, core: 2. Of those that a mesh axis runs over, the one named last changes fastest.
Arguments:
- features: bfloat16 [32, 16, 4096, 128], P(('grp', 'lon')), parts along dimension 0, may hold values from -6 to 6
- conv_weight: bfloat16 [3, 3, 128, 64], replicated, may hold values from -0.1875 to 0.1875
- conv_bias: float32 [64], replicated, may hold values from -3 to 3
- head_weight: bfloat16 [64, 4], replicated, may hold values from -0.75 to 0.75
- head_bias: float32 [4], replicated, may hold values from -3 to 3
Outputs:
- peak_margin: float32 [32, 16, 4096], P(('grp', 'lon')), parts along dimension 0
- regress: float32 [32, 3, 16, 4096], P(('grp', 'lon')), parts along dimension 0
There are 2 independent parts, one for each index of `grp`. A program takes and returns all parts, laid end to end along the dimension named above; an argument that names none is the same for every part. Nothing has to cross between parts.
All inputs are finite; a program needn't handle non-finite values.
Results may differ from a plain program's by a relative error of at most 0.008.
Values may be sent and summed in bfloat16 or wider, within the bound.
A program may use at most 384 MiB of HBM per device.

v0:
```python
from functools import reduce

import jax
import jax.numpy as jnp
from jax import lax
from jax.sharding import PartitionSpec as P

LATT = 4


def from_behind(array, axis, by):
    peers = lax.axis_size(axis)
    return lax.ppermute(array, axis, [(i, (i + by) % peers) for i in range(peers)])


def feature_lon(rim_piece, distance):
    return from_behind(rim_piece, "lon", distance)


def feature_lat(rim_piece, distance):
    return from_behind(rim_piece, "lon", distance)


def heat_lon(rim_piece, distance):
    return from_behind(rim_piece, "lon", distance)


def heat_lat(rim_piece, distance):
    return from_behind(rim_piece, "lon", distance)


def latitude_of_tile():
    return (lax.axis_index("lon") + 1) % LATT


def lon_extend(tile_in, rim_width, lon_move):
    col_count = tile_in.shape[1]
    west_rim = lon_move(tile_in[:, col_count - rim_width :], LATT)
    east_rim = lon_move(tile_in[:, :rim_width], -LATT)
    return jnp.concatenate([west_rim, tile_in, east_rim], axis=1)


def lat_extend(wide_tile, rim_width, lat_move):
    row_count = wide_tile.shape[0]
    lat_tile = latitude_of_tile()
    north_rim = lat_move(wide_tile[row_count - rim_width :], 1)
    south_rim = lat_move(wide_tile[:rim_width], -1)
    north_rim = jnp.where(lat_tile == 0, jnp.zeros_like(north_rim), north_rim)
    south_rim = jnp.where(lat_tile == LATT - 1, jnp.zeros_like(south_rim), south_rim)
    return jnp.concatenate([north_rim, wide_tile, south_rim], axis=0)


def lat_partial(rows, weight_tap, col_count):
    row_total = rows.shape[0]
    chans = rows.shape[2]
    hid_count = weight_tap.shape[2]
    stacked = jnp.transpose(weight_tap, (1, 0, 2)).reshape(chans, 3 * hid_count)
    product = jnp.dot(
        rows.reshape(row_total * (col_count + 2), chans),
        stacked,
        preferred_element_type=jnp.float32,
    )
    product = product.reshape(row_total, col_count + 2, 3, hid_count)
    summed = product[:, 0:col_count, 0] + product[:, 1 : col_count + 1, 1]
    summed = summed + product[:, 2 : col_count + 2, 2]
    return summed.astype(jnp.bfloat16)


def suppress(heat_pad, row_count, col_count):
    full_max = reduce(jnp.maximum, [heat_pad[:, sx : sx + col_count] for sx in range(9)])
    side_max = reduce(
        jnp.maximum,
        [heat_pad[4 : 4 + row_count, sx : sx + col_count] for sx in range(9) if sx != 4],
    )
    others = reduce(jnp.maximum, [full_max[sy : sy + row_count] for sy in range(9) if sy != 4])
    return heat_pad[4 : 4 + row_count, 4 : 4 + col_count] - jnp.maximum(others, side_max)


def shards(features, conv_weight, conv_bias, head_weight, head_bias):
    tile_in = features[0]
    row_count = tile_in.shape[0]
    col_count = tile_in.shape[1]
    wide_tile = lon_extend(tile_in, 1, feature_lon)
    padded = lat_extend(wide_tile, 1, feature_lat)
    parts = [
        lat_partial(padded[tap : tap + row_count], conv_weight[tap], col_count) for tap in range(3)
    ]
    pre_act = conv_bias
    for part_sum in parts:
        pre_act = pre_act + part_sum.astype(jnp.float32)
    hidden = jax.nn.relu(pre_act).astype(jnp.bfloat16)
    logits = jnp.einsum("kj,hwk->jhw", head_weight, hidden, preferred_element_type=jnp.float32)
    logits = logits + head_bias[:, None, None]
    heatmap = jax.nn.sigmoid(logits[0])
    heat_pad = lat_extend(lon_extend(heatmap, 4, heat_lon), 4, heat_lat)
    peak_margin = suppress(heat_pad, row_count, col_count)
    return (peak_margin[None], logits[1:][None])


def solution(mesh):
    in_specs = (P(("grp", "lon"), None, None, None), P(), P(), P(), P())
    out_specs = (P(("grp", "lon"), None, None), P(("grp", "lon"), None, None, None))
    return jax.shard_map(shards, mesh=mesh, in_specs=in_specs, out_specs=out_specs, check_vma=False)
```

profile of v0, /device:TPU:0, one launch (start us, length us, event | category | flops | bytes accessed | tf_op | source)
XLA Modules:
  0.0 232.7 jit_solution(13371337372147883804)
XLA Ops:
  0.6 0.0 copy-start
  0.6 0.8 fusion.52
  1.4 5.1 %collective-permute-start.1 = (bf16[16,1,128]{2,1,0:T(2,128)(2,1)S(1)}, bf16[16,1,128]{2,1,0:T(2,128)(2,1)S(1)}, u32[]{:S(2)}, u32[]{:S(2)}) collective-permute-start(bf16[16,1,128]{2,1,0:T(2,128)(2,1)S(1)} %get-tuple-element.6), channel_id=1, source_target_pairs={{0,12},{1,13},{2,14},{3,15},{4,0},{5,1},{6,2},{7,3},{8,4},{9,5},{1... | collective-permute-start | bytes 12296 | tf_op jit(solution)/shard_map/ppermute | solution.py:13
  6.6 1.4 collective-permute-done.1
  7.9 4.1 %collective-permute-done = bf16[16,1,128]{2,1,0:T(2,128)(2,1)S(1)} collective-permute-done((bf16[16,1,128]{2,1,0:T(2,128)(2,1)S(1)}, bf16[16,1,128]{2,1,0:T(2,128)(2,1)S(1)}, u32[]{:S(2)}, u32[]{:S(2)}) %collective-permute-start) | collective-permute-done | bytes 4128 | tf_op jit(solution)/shard_map/ppermute | solution.py:13
  12.0 81.2 %concatenate.28 = bf16[16,4098,128]{2,1,0:T(8,128)(2,1)} concatenate(bf16[16,1,128]{2,1,0:T(2,128)(2,1)S(1)} %collective-permute-done, bf16[16,4096,128]{2,1,0:T(8,128)(2,1)} %bitcast.96, bf16[16,1,128]{2,1,0:T(2,128)(2,1)S(1)} %collective-permute-done.1), dimensions={1} | concatenate | bytes 33570816 | tf_op jit(solution)/shard_map/concatenate | solution.py:40
  93.2 1.7 fusion.51
  94.9 0.1 collective-permute-start.3
  95.0 0.5 collective-permute-start.2
  95.5 23.5 %fusion.8 = f32[16,4098,3,64]{1,3,0,2:T(8,128)} fusion(bf16[16,4098,128]{2,1,0:T(8,128)(2,1)} %concatenate.28, bf16[3,3,128,64]{2,3,1,0:T(8,128)(2,1)S(1)} %copy-done.1), kind=kOutput, calls=%fused_computation.8 | convolution fusion | flops 3222798336 | bytes 67190784 | tf_op jit(solution)/shard_map/dot_general | solution.py:58
  119.0 0.2 broadcast_select_fusion.1
  119.2 22.9 %fusion.5 = f32[16,4098,3,64]{1,3,2,0:T(8,128)} fusion(bf16[16,4098,128]{2,1,0:T(8,128)(2,1)} %concatenate.28, bf16[1,4098,128]{2,1,0:T(8,128)(2,1)S(1)} %broadcast_select_fusion.1, bf16[3,3,128,64]{2,3,1,0:T(8,128)(2,1)S(1)} %copy-done.1), kind=kOutput, calls=%fused_computation.6 | convolution fusion | flops 3256369152 | bytes 68241408 | tf_op jit(solution)/shard_map/dot_general | solution.py:58
  142.1 0.2 broadcast_select_fusion
  142.4 0.0 copy-start.3
  142.4 23.0 %fusion.1 = f32[16,4098,3,64]{1,3,0,2:T(8,128)} fusion(bf16[1,4098,128]{2,1,0:T(8,128)(2,1)S(1)} %broadcast_select_fusion, bf16[16,4098,128]{2,1,0:T(8,128)(2,1)} %concatenate.28, bf16[3,3,128,64]{2,3,1,0:T(8,128)(2,1)S(1)} %copy-done.1), kind=kOutput, calls=%fused_computation.2 | convolution fusion | flops 3256369152 | bytes 68241408 | tf_op jit(solution)/shard_map/dot_general | solution.py:58
  165.3 49.6 %fusion.58 = bf16[16,4096,64]{1,2,0:T(8,128)(2,1)S(1)} fusion(f32[16,4098,3,64]{1,3,2,0:T(8,128)} %fusion.5, f32[16,4098,3,64]{1,3,0,2:T(8,128)} %fusion.8, f32[16,4098,3,64]{1,3,0,2:T(8,128)} %fusion.1, f32[64]{0:T(128)S(1)} %copy-done.3), kind=kLoop, calls=%fused_computation.21.clone.clone.1 | loop fusion | flops 71303168 | bytes 159383808 | tf_op jit(solution)/shard_map/kj,hwk->jhw/dot_general | solution.py:92
  214.9 1.6 fusion.18
  216.6 0.6 fusion.20
  217.2 0.1 fusion.40
  217.3 0.1 fusion.54
  217.4 0.5 collective-permute-start.4
  217.8 3.3 %collective-permute-start.5 = (f32[16,4]{1,0:T(8,128)S(1)}, f32[16,4]{1,0:T(8,128)S(1)}, u32[]{:S(2)}, u32[]{:S(2)}) collective-permute-start(f32[16,4]{1,0:T(8,128)S(1)} %get-tuple-element.11), channel_id=1, source_target_pairs={{0,12},{1,13},{2,14},{3,15},{4,0},{5,1},{6,2},{7,3},{8,4},{9,5},{1... | collective-permute-start | bytes 776 | tf_op jit(solution)/shard_map/ppermute | solution.py:13
  221.2 1.6 collective-permute-done.4
  222.8 0.2 concatenate.31
  223.0 0.2 collective-permute-start.6
  223.2 0.9 slice_bitcast_fusion
  224.1 4.3 %collective-permute-start.7 = (f32[4,4104]{1,0:T(4,128)S(1)}, f32[4,4104]{1,0:T(4,128)S(1)}, u32[]{:S(2)}, u32[]{:S(2)}) collective-permute-start(f32[4,4104]{1,0:T(4,128)S(1)} %get-tuple-element.9), channel_id=1, source_target_pairs={{0,15},{1,0},{2,1},{3,2},{4,3},{5,4},{6,5},{7,6},{8,7},{9,8},{10,9... | collective-permute-start | bytes 197000 | tf_op jit(solution)/shard_map/ppermute | solution.py:13
  228.5 1.0 collective-permute-done.6
  229.5 0.9 collective-permute-done.7
  230.4 0.1 pad_maximum_fusion.2
  230.5 0.9 slice_maximum_fusion
  231.3 1.3 fusion.26
  (13 shorter events, 0.1 us)
Async XLA Ops:
  0.6 214.3 %copy-start = (bf16[64,4]{0,1:T(4,128)(2,1)S(1)}, bf16[64,4]{0,1:T(4,128)(2,1)}, u32[]{:S(2)}) copy-start(bf16[64,4]{0,1:T(4,128)(2,1)} %param.8) | copy-start | bytes 1540
  1.4 6.5 %collective-permute-start.1 = (bf16[16,1,128]{2,1,0:T(2,128)(2,1)S(1)}, bf16[16,1,128]{2,1,0:T(2,128)(2,1)S(1)}, u32[]{:S(2)}, u32[]{:S(2)}) collective-permute-start(bf16[16,1,128]{2,1,0:T(2,128)(2,1)S(1)} %get-tuple-element.6), channel_id=1, source_target_pairs={{0,12},{1,13},{2,14},{3,15},{4,0},{5,1},{6,2},{7,3},{8,4},{9,5},{1... | collective-permute-start | bytes 12296 | tf_op jit(solution)/shard_map/ppermute | solution.py:13
  6.5 5.4 %collective-permute-start = (bf16[16,1,128]{2,1,0:T(2,128)(2,1)S(1)}, bf16[16,1,128]{2,1,0:T(2,128)(2,1)S(1)}, u32[]{:S(2)}, u32[]{:S(2)}) collective-permute-start(bf16[16,1,128]{2,1,0:T(2,128)(2,1)S(1)} %get-tuple-element.7), channel_id=1, source_target_pairs={{0,4},{1,5},{2,6},{3,7},{4,8},{5,9},{6,10},{7,11},{8,12},{9,13},{1... | collective-permute-start | bytes 12296 | tf_op jit(solution)/shard_map/ppermute | solution.py:13
  6.5 88.9 %copy-start.1 = (bf16[3,3,128,64]{2,3,1,0:T(8,128)(2,1)S(1)}, bf16[3,3,128,64]{2,3,1,0:T(8,128)(2,1)}, u32[]{:S(2)}) copy-start(bf16[3,3,128,64]{2,3,1,0:T(8,128)(2,1)} %param.6) | copy-start | bytes 442372
  94.9 47.2 %collective-permute-start.3 = (bf16[1,4098,128]{2,1,0:T(8,128)(2,1)S(1)}, bf16[1,4098,128]{2,1,0:T(8,128)(2,1)S(1)}, u32[]{:S(2)}, u32[]{:S(2)}) collective-permute-start(bf16[1,4098,128]{2,1,0:T(8,128)(2,1)S(1)} %get-tuple-element.4), channel_id=1, source_target_pairs={{0,15},{1,0},{2,1},{3,2},{4,3},{5,4},{6,5},{7,6},{8,7},{9,8},{10,9... | collective-permute-start | bytes 3147272 | tf_op jit(solution)/shard_map/ppermute | solution.py:13
  95.0 24.0 %collective-permute-start.2 = (bf16[1,4098,128]{2,1,0:T(8,128)(2,1)S(1)}, bf16[1,4098,128]{2,1,0:T(8,128)(2,1)S(1)}, u32[]{:S(2)}, u32[]{:S(2)}) collective-permute-start(bf16[1,4098,128]{2,1,0:T(8,128)(2,1)S(1)} %get-tuple-element.5), channel_id=1, source_target_pairs={{0,1},{1,2},{2,3},{3,4},{4,5},{5,6},{6,7},{7,8},{8,9},{9,10},{10,1... | collective-permute-start | bytes 3147272 | tf_op jit(solution)/shard_map/ppermute | solution.py:13
  142.4 23.0 %copy-start.3 = (f32[64]{0:T(128)S(1)}, f32[64]{0:T(128)}, u32[]{:S(2)}) copy-start(f32[64]{0:T(128)} %param.7) | copy-start | bytes 772
  165.3 51.2 %copy-start.2 = (f32[4]{0:T(128)S(1)}, f32[4]{0:T(128)}, u32[]{:S(2)}) copy-start(f32[4]{0:T(128)} %param.9) | copy-start | bytes 52
  217.4 5.5 %collective-permute-start.4 = (f32[16,4]{1,0:T(8,128)S(1)}, f32[16,4]{1,0:T(8,128)S(1)}, u32[]{:S(2)}, u32[]{:S(2)}) collective-permute-start(f32[16,4]{1,0:T(8,128)S(1)} %get-tuple-element.10), channel_id=1, source_target_pairs={{0,4},{1,5},{2,6},{3,7},{4,8},{5,9},{6,10},{7,11},{8,12},{9,13},{1... | collective-permute-start | bytes 776 | tf_op jit(solution)/shard_map/ppermute | solution.py:13
  217.8 5.0 %collective-permute-start.5 = (f32[16,4]{1,0:T(8,128)S(1)}, f32[16,4]{1,0:T(8,128)S(1)}, u32[]{:S(2)}, u32[]{:S(2)}) collective-permute-start(f32[16,4]{1,0:T(8,128)S(1)} %get-tuple-element.11), channel_id=1, source_target_pairs={{0,12},{1,13},{2,14},{3,15},{4,0},{5,1},{6,2},{7,3},{8,4},{9,5},{1... | collective-permute-start | bytes 776 | tf_op jit(solution)/shard_map/ppermute | solution.py:13
  223.0 6.5 %collective-permute-start.6 = (f32[4,4104]{1,0:T(4,128)S(1)}, f32[4,4104]{1,0:T(4,128)S(1)}, u32[]{:S(2)}, u32[]{:S(2)}) collective-permute-start(f32[4,4104]{1,0:T(4,128)S(1)} %get-tuple-element.8), channel_id=1, source_target_pairs={{0,1},{1,2},{2,3},{3,4},{4,5},{5,6},{6,7},{7,8},{8,9},{9,10},{10,1... | collective-permute-start | bytes 197000 | tf_op jit(solution)/shard_map/ppermute | solution.py:13
  224.1 6.3 %collective-permute-start.7 = (f32[4,4104]{1,0:T(4,128)S(1)}, f32[4,4104]{1,0:T(4,128)S(1)}, u32[]{:S(2)}, u32[]{:S(2)}) collective-permute-start(f32[4,4104]{1,0:T(4,128)S(1)} %get-tuple-element.9), channel_id=1, source_target_pairs={{0,15},{1,0},{2,1},{3,2},{4,3},{5,4},{6,5},{7,6},{8,7},{9,8},{10,9... | collective-permute-start | bytes 197000 | tf_op jit(solution)/shard_map/ppermute | solution.py:13
where the time goes:
time: 236 us; the launch traced here: 233 us
  local copies, waits for them, and re-layouts  84.9 us (36%)
  matrix products  71.1 us (30%)
  other arithmetic  53 us (22%)
  starting transfers between devices  14 us (6%)
  waiting for transfers between devices  8.98 us (4%)
    concatenate x2, local copies, waits for them, and re-layouts, lon_extend(): return jnp.concatenate([west_rim, tile_in, east_rim], axis=1)  81.4 us
    dot_general x3, matrix products, lat_partial(): jnp.dot(rows.reshape(row_total * (col_count + 2), chans), stacked, prefer...  69.4 us
    dot_general x1, other arithmetic, shards(): jnp.einsum('kj,hwk->jhw', head_weight, hidden, preferred_element_type=jnp...  49.6 us
    ppermute x8, starting transfers between devices, from_behind(): lax.ppermute(array, axis, [(i, (i + by) % peers) for i in range(peers)])  14 us
    ppermute x8, waiting for transfers between devices, from_behind(): lax.ppermute(array, axis, [(i, (i + by) % peers) for i in range(peers)])  8.98 us
  transfers between devices with their start and end apart: 8, of which 5 were waited for; matrix products, arithmetic and copies ran while one was open for 20% of the time, Pallas kernels for 0%

commit v1 on v0

v1 whole, which is shorter than its diff:
```python
import jax
import jax.numpy as jnp
from jax import lax
from jax.experimental import pallas as pl
from jax.experimental.pallas import tpu as pltpu
from jax.sharding import PartitionSpec as P

LATT = 4
CB = 512
PAD = 16
LANES = 128
MESH = pl.DeviceIdType.MESH


def kernel(
    n, x_ref, cw_ref, cb_ref, hw_ref, hb_ref, margin_ref, regress_ref,
    xbuf, wbuf, hbig, pre_edge, hid, lg, sendbuf, recvbuf, hs,
    x_sem, rim_send, rim_recv, lat_send, lat_recv, heat_send, heat_recv,
):
    rows, cols = xbuf.shape[0], xbuf.shape[1] - 2 * PAD
    pairs = rows // 2
    blocks = cols // CB
    half = CB // 2
    t = lax.axis_index("lon")
    lat = lax.rem(t + 1, LATT)
    has_north = lat != 0
    has_south = lat != LATT - 1
    grp = lax.axis_index("grp")

    def dev(shift):
        return (grp, lax.rem(t + shift + n, n))

    north, south, west, east = dev(-1), dev(1), dev(-LATT), dev(LATT)

    def own_copy(c):
        start = pl.multiple_of(c * CB, CB)
        return pltpu.make_async_copy(
            x_ref.at[0, :, pl.ds(start, CB)],
            xbuf.at[:, pl.ds(PAD + start, CB)],
            x_sem.at[c],
        )

    for c in range(blocks):
        own_copy(c).start()

    barrier = pltpu.get_barrier_semaphore()

    def greet(target):
        pl.semaphore_signal(barrier, inc=1, device_id=target, device_id_type=MESH)

    greet(west)
    greet(east)

    @pl.when(has_north)
    def _():
        greet(north)
        greet(dev(-1 - LATT))
        greet(dev(-1 + LATT))

    @pl.when(has_south)
    def _():
        greet(south)
        greet(dev(1 - LATT))
        greet(dev(1 + LATT))

    zero_tap = jnp.zeros((LANES, 64), jnp.bfloat16)

    def tap(a, b):
        return cw_ref[a, b] if 0 <= a <= 2 else zero_tap

    for b in range(3):
        for s in range(2):
            lo = (b * 2 + s) * LANES
            wbuf[lo : lo + LANES, 0:LANES] = jnp.concatenate([tap(s + 1, b), tap(s, b)], axis=1)
            wbuf[lo : lo + LANES, LANES : 2 * LANES] = jnp.concatenate(
                [tap(s - 1, b), tap(s + 2, b)], axis=1
            )
    spread = (
        lax.broadcasted_iota(jnp.int32, (4 * rows, 4), 0) // rows
        == lax.broadcasted_iota(jnp.int32, (4 * rows, 4), 1)
    )
    spread = jnp.where(spread, 1.0, 0.0).astype(jnp.bfloat16)
    by_row = lax.dot_general(
        spread, hw_ref[...], (((1,), (1,)), ((), ())), preferred_element_type=jnp.float32
    )
    wide = jnp.concatenate([by_row] * rows, axis=1)
    keep = (
        lax.rem(lax.broadcasted_iota(jnp.int32, wide.shape, 0), rows)
        == lax.broadcasted_iota(jnp.int32, wide.shape, 1) // 64
    )
    hbig[...] = jnp.where(keep, wide, 0.0).astype(jnp.bfloat16)

    @pl.when(jnp.logical_not(has_north))
    def _():
        recvbuf[0] = jnp.zeros(recvbuf.shape[1:], recvbuf.dtype)
        hs[0:8, :] = jnp.zeros((8, hs.shape[1]), hs.dtype)

    @pl.when(jnp.logical_not(has_south))
    def _():
        recvbuf[1] = jnp.zeros(recvbuf.shape[1:], recvbuf.dtype)
        hs[8 + rows : 16 + rows, :] = jnp.zeros((8, hs.shape[1]), hs.dtype)

    peers = 2 + jnp.where(has_north, 3, 0) + jnp.where(has_south, 3, 0)
    pl.semaphore_wait(barrier, peers)

    def remote(src, dst, send, recv, target):
        return pltpu.make_async_remote_copy(
            src_ref=src, dst_ref=dst, send_sem=send, recv_sem=recv,
            device_id=target, device_id_type=MESH,
        )

    to_east = remote(
        x_ref.at[0, :, pl.ds(cols - PAD, PAD)], xbuf.at[:, pl.ds(0, PAD)],
        rim_send.at[0], rim_recv.at[0], east,
    )
    to_west = remote(
        x_ref.at[0, :, pl.ds(0, PAD)], xbuf.at[:, pl.ds(cols + PAD, PAD)],
        rim_send.at[1], rim_recv.at[1], west,
    )
    to_east.start()
    to_west.start()

    low_lane = lax.broadcasted_iota(jnp.int32, (1, LANES), 1) < 64
    bias = jnp.concatenate([cb_ref[...], cb_ref[...]], axis=1)

    def lat_copy(way, c):
        part = pl.ds(pl.multiple_of(c * half, half), half)
        return remote(
            sendbuf.at[way, part], recvbuf.at[way, part],
            lat_send.at[way, c], lat_recv.at[way, c], south if way == 0 else north,
        )

    own_copy(0).wait()
    own_copy(1).wait()

    def first(i, carry):
        c = lax.rem(i + 1, blocks)
        base = pl.multiple_of(c * CB, CB)

        @pl.when(i + 2 < blocks)
        def _():
            own_copy(i + 2).wait()

        @pl.when(i == blocks - 2)
        def _():
            to_west.wait_recv()

        @pl.when(i == blocks - 1)
        def _():
            to_east.wait_recv()

        def products(p):
            win = jnp.concatenate(
                [xbuf[2 * p, pl.ds(base, CB + 2 * PAD)], xbuf[2 * p + 1, pl.ds(base, CB + 2 * PAD)]],
                axis=1,
            )
            taps = jnp.concatenate(
                [win[PAD - 1 + b : PAD - 1 + b + CB] for b in range(3)], axis=1
            )
            return jnp.dot(taps, wbuf[...], preferred_element_type=jnp.float32)

        def finish(p, main, above, below):
            pre = main + bias
            if p == 0:
                pre_edge[0, pl.ds(base, CB)] = pre + jnp.where(low_lane, 0.0, below)
            elif p == pairs - 1:
                pre_edge[1, pl.ds(base, CB)] = pre + jnp.where(low_lane, above, 0.0)
            else:
                pre = pre + jnp.where(low_lane, above, below)
                at = (p - 1) * LANES
                hid[:, at : at + LANES] = jnp.maximum(pre, 0.0).astype(jnp.bfloat16)

        before = None
        held = None
        for p in range(pairs):
            out = products(p)
            main, side = out[:, :LANES], out[:, LANES:]
            if p == 0:
                packed = jnp.where(low_lane, pltpu.roll(side[:half], 64, 1), side[half:])
                sendbuf[1, pl.ds(pl.multiple_of(c * half, half), half)] = packed.astype(jnp.bfloat16)
            else:
                finish(p - 1, held[0], before, side)
                before = held[1]
            held = (main, side)
        packed = jnp.where(low_lane, held[1][:half], pltpu.roll(held[1][half:], 64, 1))
        sendbuf[0, pl.ds(pl.multiple_of(c * half, half), half)] = packed.astype(jnp.bfloat16)
        finish(pairs - 1, held[0], before, None)

        @pl.when(has_south)
        def _():
            lat_copy(0, c).start()

        @pl.when(has_north)
        def _():
            lat_copy(1, c).start()

        lg[:, pl.ds(base, CB)] = lax.dot_general(
            hbig[:, LANES : (pairs - 1) * LANES], hid[...],
            (((1,), (1,)), ((), ())), preferred_element_type=jnp.float32,
        )
        return carry

    lax.fori_loop(0, blocks, first, 0)

    def second(i, carry):
        c = lax.rem(i + 1, blocks)
        base = pl.multiple_of(c * CB, CB)
        part = pl.ds(pl.multiple_of(c * half, half), half)

        @pl.when(has_north)
        def _():
            lat_copy(0, c).wait_recv()

        @pl.when(has_south)
        def _():
            lat_copy(1, c).wait_recv()

        above = recvbuf[0, part].astype(jnp.float32)
        above = jnp.concatenate([above, pltpu.roll(above, 64, 1)], axis=0)
        below = recvbuf[1, part].astype(jnp.float32)
        below = jnp.concatenate([pltpu.roll(below, 64, 1), below], axis=0)
        top = pre_edge[0, pl.ds(base, CB)] + jnp.where(low_lane, above, 0.0)
        bottom = pre_edge[1, pl.ds(base, CB)] + jnp.where(low_lane, 0.0, below)
        edge = jnp.maximum(jnp.concatenate([top, bottom], axis=1), 0.0).astype(jnp.bfloat16)
        heads = jnp.concatenate([hbig[:, :LANES], hbig[:, (pairs - 1) * LANES :]], axis=1)
        logits = lg[:, pl.ds(base, CB)] + lax.dot_general(
            heads, edge, (((1,), (1,)), ((), ())), preferred_element_type=jnp.float32
        )
        hs[8 : 8 + rows, pl.ds(LANES + base, CB)] = jax.nn.sigmoid(logits[:rows] + hb_ref[0])
        for k in range(1, 4):
            regress_ref[0, k - 1, :, pl.ds(base, CB)] = (
                logits[k * rows : (k + 1) * rows] + hb_ref[k]
            )
        return carry

    lax.fori_loop(0, blocks, second, 0)

    own, far = pl.ds(8, rows), pl.ds(LANES + cols, LANES)
    first_cols, last_cols = pl.ds(LANES, LANES), pl.ds(cols, LANES)
    near = pl.ds(0, LANES)
    mid = pl.ds(LANES, cols)
    first_rows, last_rows = pl.ds(8, 8), pl.ds(rows, 8)
    over, under = pl.ds(0, 8), pl.ds(8 + rows, 8)

    def heat(k, src, dst, target):
        return remote(hs.at[src], hs.at[dst], heat_send.at[k], heat_recv.at[k], target)

    lon_heat = [
        heat(0, (own, last_cols), (own, near), east),
        heat(1, (own, first_cols), (own, far), west),
    ]
    down_heat = [
        heat(2, (last_rows, mid), (over, mid), south),
        heat(3, (last_rows, last_cols), (over, near), dev(1 + LATT)),
        heat(4, (last_rows, first_cols), (over, far), dev(1 - LATT)),
    ]
    up_heat = [
        heat(5, (first_rows, mid), (under, mid), north),
        heat(6, (first_rows, last_cols), (under, near), dev(-1 + LATT)),
        heat(7, (first_rows, first_cols), (under, far), dev(-1 - LATT)),
    ]

    @pl.when(has_south)
    def _():
        for copy in down_heat:
            copy.start()

    @pl.when(has_north)
    def _():
        for copy in up_heat:
            copy.start()

    for copy in lon_heat:
        copy.start()

    to_east.wait_send()
    to_west.wait_send()

    @pl.when(has_south)
    def _():
        lax.fori_loop(0, blocks, lambda c, z: (lat_copy(0, c).wait_send(), z)[1], 0)

    @pl.when(has_north)
    def _():
        lax.fori_loop(0, blocks, lambda c, z: (lat_copy(1, c).wait_send(), z)[1], 0)

    for copy in lon_heat:
        copy.wait_recv()

    @pl.when(has_north)
    def _():
        for copy in down_heat:
            copy.wait_recv()

    @pl.when(has_south)
    def _():
        for copy in up_heat:
            copy.wait_recv()

    def peaks(i, carry):
        base = pl.multiple_of(i * CB, CB)
        h = hs[:, pl.ds(base, CB + 2 * LANES)]
        width = CB + 2 * LANES

        def ahead(v, k):
            return pltpu.roll(v, (width - k) % width, 1)

        m = jnp.maximum(h, ahead(h, 1))
        m = jnp.maximum(m, ahead(m, 2))
        sides = jnp.maximum(ahead(m, width - 4), ahead(m, 1))
        sides = sides[:, LANES : LANES + CB]
        center = h[:, LANES : LANES + CB]
        full = jnp.maximum(sides, center)
        height = full.shape[0]
        v = jnp.maximum(full, pltpu.roll(full, height - 1, 0))
        v = jnp.maximum(v, pltpu.roll(v, height - 2, 0))
        others = jnp.maximum(pltpu.roll(v, 4, 0), pltpu.roll(v, height - 1, 0))
        around = jnp.maximum(others, sides)
        margin_ref[0, :, pl.ds(base, CB)] = (center - around)[8 : 8 + rows]
        return carry

    lax.fori_loop(0, blocks, peaks, 0)

    for copy in lon_heat:
        copy.wait_send()

    @pl.when(has_south)
    def _():
        for copy in down_heat:
            copy.wait_send()

    @pl.when(has_north)
    def _():
        for copy in up_heat:
            copy.wait_send()


def solution(mesh):
    n = mesh.shape["lon"]

    def shards(features, conv_weight, conv_bias, head_weight, head_bias):
        _, rows, cols, chans = features.shape
        pairs = rows // 2
        blocks = cols // CB
        vmem = pl.BlockSpec(memory_space=pltpu.VMEM)
        return pl.pallas_call(
            lambda *refs: kernel(n, *refs),
            out_shape=(
                jax.ShapeDtypeStruct((1, rows, cols), jnp.float32),
                jax.ShapeDtypeStruct((1, 3, rows, cols), jnp.float32),
            ),
            in_specs=[
                pl.BlockSpec(memory_space=pl.ANY), vmem, vmem, vmem,
                pl.BlockSpec(memory_space=pltpu.SMEM),
            ],
            out_specs=(vmem, vmem),
            scratch_shapes=[
                pltpu.VMEM((rows, cols + 2 * PAD, chans), jnp.bfloat16),
                pltpu.VMEM((6 * LANES, 2 * LANES), jnp.bfloat16),
                pltpu.VMEM((4 * rows, pairs * LANES), jnp.bfloat16),
                pltpu.VMEM((2, cols, LANES), jnp.float32),
                pltpu.VMEM((CB, (pairs - 2) * LANES), jnp.bfloat16),
                pltpu.VMEM((4 * rows, cols), jnp.float32),
                pltpu.VMEM((2, cols // 2, LANES), jnp.bfloat16),
                pltpu.VMEM((2, cols // 2, LANES), jnp.bfloat16),
                pltpu.VMEM((rows + 16, cols + 2 * LANES), jnp.float32),
                pltpu.SemaphoreType.DMA((blocks,)),
                pltpu.SemaphoreType.DMA((2,)),
                pltpu.SemaphoreType.DMA((2,)),
                pltpu.SemaphoreType.DMA((2, blocks)),
                pltpu.SemaphoreType.DMA((2, blocks)),
                pltpu.SemaphoreType.DMA((8,)),
                pltpu.SemaphoreType.DMA((8,)),
            ],
            compiler_params=pltpu.CompilerParams(
                collective_id=0, has_side_effects=True, vmem_limit_bytes=56 * 1024 * 1024
            ),
            cost_estimate=pl.CostEstimate(
                flops=2 * rows * cols * chans * 9 * 64,
                bytes_accessed=2 * rows * cols * chans,
                transcendentals=rows * cols,
            ),
        )(features, conv_weight, conv_bias[None], head_weight, head_bias)

    in_specs = (P(("grp", "lon"), None, None, None), P(), P(), P(), P())
    out_specs = (P(("grp", "lon"), None, None), P(("grp", "lon"), None, None, None))
    return jax.shard_map(shards, mesh=mesh, in_specs=in_specs, out_specs=out_specs, check_vma=False)
```

time: 236 us -> 47.3 us (0.20); the launches traced: 233 us -> 47.1 us
  local copies, waits for them, and re-layouts: 84.9 us -> 6.91 us
  matrix products: 71.1 us -> 0 us
  other arithmetic: 53 us -> 0 us
  Pallas kernels: 0 us -> 39.5 us
  starting transfers between devices: 14 us -> 0 us
  waiting for transfers between devices: 8.98 us -> 0 us
    concatenate x2 -> x0, local copies, waits for them, and re-layouts: 81.4 us -> none  [lon_extend(): return jnp.concatenate([west_rim, tile_in, east_rim], axis=1)]
    dot_general x4 -> x0, matrix products: 71.1 us -> none  [the longest x3 69.4 us: lat_partial(): jnp.dot(rows.reshape(row_total * (col_count + 2), chans), stacked, prefer...]
    dot_general x1 -> x0, other arithmetic: 49.6 us -> none  [shards(): jnp.einsum('kj,hwk->jhw', head_weight, hidden, preferred_element_type=jnp...]
    pallas_call x0 -> x1, Pallas kernels: none -> 39.5 us  [shards(): pl.pallas_call(lambda *refs: kernel(n, *refs), out_shape=(jax.ShapeDtypeS...]
    ppermute x8 -> x0, starting transfers between devices: 14 us -> none  [from_behind(): lax.ppermute(array, axis, [(i, (i + by) % peers) for i in range(peers)])]
    ppermute x8 -> x0, waiting for transfers between devices: 8.98 us -> none  [from_behind(): lax.ppermute(array, axis, [(i, (i + by) % peers) for i in range(peers)])]
    unnamed x8 -> x4, local copies, waits for them, and re-layouts: 0.02 us -> 6.91 us
    slice x4 -> x0, local copies, waits for them, and re-layouts: 2.57 us -> none  [the longest x1 1.68 us: lat_extend(): south_rim = lat_move(wide_tile[:rim_width], -1)]
  transfers between devices with their start and end apart: 8 -> 0, of which waited for: 5 -> 0; matrix products, arithmetic and copies ran while one was open for 20% -> 0% of each run, Pallas kernels for 0% -> 0%
where the time goes in v1:
time: 47.3 us; the launch traced here: 47.1 us
  Pallas kernels  39.5 us (84%)
  local copies, waits for them, and re-layouts  6.91 us (15%)
  between operations  0.64 us (1%)
    pallas_call x1, Pallas kernels, shards(): pl.pallas_call(lambda *refs: kernel(n, *refs), out_shape=(jax.ShapeDtypeS...  39.5 us
    unnamed x4, local copies, waits for them, and re-layouts  6.91 us

profile of v1, /device:TPU:0, one launch (start us, length us, event | category | flops | bytes accessed | tf_op | source)
XLA Modules:
  0.0 47.1 jit_solution(11251356665364048147)
XLA Ops:
  0.6 1.4 %copy.8.refs_3_ = bf16[64,4]{1,0:T(8,128)(2,1)} copy(bf16[64,4]{0,1:T(4,128)(2,1)} %param.8) | data formatting | bytes 1024 | tf_op args[3]
  2.0 1.8 %copy.7.refs_1_ = bf16[3,3,128,64]{3,2,1,0:T(8,128)(2,1)} copy(bf16[3,3,128,64]{2,3,1,0:T(8,128)(2,1)} %param.6) | data formatting | bytes 294912 | tf_op args[1]
  3.8 39.5 %shard_map.68 = (f32[1,16,4096]{2,1,0:T(8,128)}, f32[1,3,16,4096]{3,2,1,0:T(8,128)}) custom-call(bf16[1,16,4096,128]{3,2,1,0:T(8,128)(2,1)} %refs_0_.1, bf16[3,3,128,64]{3,2,1,0:T(8,128)(2,1)} %copy.7.refs_1_, f32[1,64]{1,0:T(1,128)} %bitcast.1, bf16[64,4]{1,0:T(8,128)(2,1)} %copy.8.refs_3_, f32[4]{0:T(128)} %refs_4_.1), custom_call_target="tpu_custom_call" | custom-call | flops 9663676416 | bytes 16777216 | tf_op jit(solution)/shard_map/pallas_call | solution.py:346
  43.4 1.7 %copy.11 = f32[1,16,4096]{2,1,0:T(8,128)} copy(f32[1,16,4096]{2,1,0:T(8,128)} %get-tuple-element.4) | data formatting | bytes 524288
  45.0 2.1 %copy.12 = f32[1,3,16,4096]{3,2,1,0:T(8,128)} copy(f32[1,3,16,4096]{3,2,1,0:T(8,128)} %get-tuple-element.5) | data formatting | bytes 1572864

commit v2 on v1

--- a/solution.py
+++ b/solution.py
@@ -63,7 +63,7 @@
         greet(dev(1 - LATT))
         greet(dev(1 + LATT))
 
-    zero_tap = jnp.zeros((LANES, 64), jnp.bfloat16)
+    zero_tap = jnp.zeros((64, LANES), jnp.bfloat16)
 
     def tap(a, b):
         return cw_ref[a, b] if 0 <= a <= 2 else zero_tap
@@ -71,18 +71,14 @@
     for b in range(3):
         for s in range(2):
             lo = (b * 2 + s) * LANES
-            wbuf[lo : lo + LANES, 0:LANES] = jnp.concatenate([tap(s + 1, b), tap(s, b)], axis=1)
-            wbuf[lo : lo + LANES, LANES : 2 * LANES] = jnp.concatenate(
-                [tap(s - 1, b), tap(s + 2, b)], axis=1
-            )
+            taps = [tap(s + 1, b), tap(s, b), tap(s - 1, b), tap(s + 2, b)]
+            wbuf[lo : lo + LANES, :] = jnp.concatenate(taps, axis=0).T
     spread = (
         lax.broadcasted_iota(jnp.int32, (4 * rows, 4), 0) // rows
         == lax.broadcasted_iota(jnp.int32, (4 * rows, 4), 1)
     )
     spread = jnp.where(spread, 1.0, 0.0).astype(jnp.bfloat16)
-    by_row = lax.dot_general(
-        spread, hw_ref[...], (((1,), (1,)), ((), ())), preferred_element_type=jnp.float32
-    )
+    by_row = jnp.dot(spread, hw_ref[...], preferred_element_type=jnp.float32)
     wide = jnp.concatenate([by_row] * rows, axis=1)
     keep = (
         lax.rem(lax.broadcasted_iota(jnp.int32, wide.shape, 0), rows)
@@ -380,7 +376,7 @@
                 bytes_accessed=2 * rows * cols * chans,
                 transcendentals=rows * cols,
             ),
-        )(features, conv_weight, conv_bias[None], head_weight, head_bias)
+        )(features, jnp.swapaxes(conv_weight, 2, 3), conv_bias[None], head_weight.T, head_bias)
 
     in_specs = (P(("grp", "lon"), None, None, None), P(), P(), P(), P())
     out_specs = (P(("grp", "lon"), None, None), P(("grp", "lon"), None, None, None))

time: 47.3 us -> 44.1 us (0.932)
  local copies, waits for them, and re-layouts: 6.91 us -> 3.73 us
    unnamed x4 -> x2, local copies, waits for them, and re-layouts: 6.91 us -> 3.73 us
where the time goes in v2:
time: 44.1 us; the launch traced here: 43.9 us
  Pallas kernels  39.5 us (90%)
  local copies, waits for them, and re-layouts  3.73 us (8%)
  between operations  0.64 us (1%)
    pallas_call x1, Pallas kernels, shards(): pl.pallas_call(lambda *refs: kernel(n, *refs), out_shape=(jax.ShapeDtypeS...  39.5 us
    unnamed x2, local copies, waits for them, and re-layouts  3.73 us

profile of v2, /device:TPU:0, one launch (start us, length us, event | category | flops | bytes accessed | tf_op | source)
XLA Modules:
  0.0 43.9 jit_solution(10970977363804608371)
XLA Ops:
  0.6 39.5 %shard_map.68 = (f32[1,16,4096]{2,1,0:T(8,128)}, f32[1,3,16,4096]{3,2,1,0:T(8,128)}) custom-call(bf16[1,16,4096,128]{3,2,1,0:T(8,128)(2,1)} %refs_0_.1, bf16[3,3,64,128]{3,2,1,0:T(8,128)(2,1)} %bitcast.3, f32[1,64]{1,0:T(1,128)} %bitcast.5, bf16[4,64]{1,0:T(4,128)(2,1)} %bitcast.4, f32[4]{0:T(128)} %refs_4_.1), custom_call_target="tpu_custom_call" | custom-call | flops 9663676416 | bytes 16777216 | tf_op jit(solution)/shard_map/pallas_call | solution.py:342
  40.1 1.7 %copy.9 = f32[1,16,4096]{2,1,0:T(8,128)} copy(f32[1,16,4096]{2,1,0:T(8,128)} %get-tuple-element.4) | data formatting | bytes 524288
  41.8 2.1 %copy.10 = f32[1,3,16,4096]{3,2,1,0:T(8,128)} copy(f32[1,3,16,4096]{3,2,1,0:T(8,128)} %get-tuple-element.5) | data formatting | bytes 1572864

commit v3 on v2

--- a/solution.py
+++ b/solution.py
@@ -224,9 +224,7 @@
         )
         hs[8 : 8 + rows, pl.ds(LANES + base, CB)] = jax.nn.sigmoid(logits[:rows] + hb_ref[0])
         for k in range(1, 4):
-            regress_ref[0, k - 1, :, pl.ds(base, CB)] = (
-                logits[k * rows : (k + 1) * rows] + hb_ref[k]
-            )
+            regress_ref[0, k - 1, :, pl.ds(base, CB)] = logits[k * rows : (k + 1) * rows]
         return carry
 
     lax.fori_loop(0, blocks, second, 0)
@@ -331,6 +329,12 @@
             copy.wait_send()
 
 
+def deliver(margin_in, raw_in, hb_ref, margin_out, regress_out):
+    margin_out[...] = margin_in[...]
+    for k in range(1, 4):
+        regress_out[0, k - 1] = raw_in[0, k - 1] + hb_ref[k]
+
+
 def solution(mesh):
     n = mesh.shape["lon"]
 
@@ -339,7 +343,7 @@
         pairs = rows // 2
         blocks = cols // CB
         vmem = pl.BlockSpec(memory_space=pltpu.VMEM)
-        return pl.pallas_call(
+        margin, raw = pl.pallas_call(
             lambda *refs: kernel(n, *refs),
             out_shape=(
                 jax.ShapeDtypeStruct((1, rows, cols), jnp.float32),
@@ -377,6 +381,19 @@
                 transcendentals=rows * cols,
             ),
         )(features, jnp.swapaxes(conv_weight, 2, 3), conv_bias[None], head_weight.T, head_bias)
+        span = cols // 2
+        margin_spec = pl.BlockSpec((1, rows, span), lambda i: (0, 0, i))
+        regress_spec = pl.BlockSpec((1, 3, rows, span), lambda i: (0, 0, 0, i))
+        return pl.pallas_call(
+            deliver,
+            grid=(2,),
+            out_shape=(
+                jax.ShapeDtypeStruct(margin.shape, jnp.float32),
+                jax.ShapeDtypeStruct(raw.shape, jnp.float32),
+            ),
+            in_specs=[margin_spec, regress_spec, pl.BlockSpec(memory_space=pltpu.SMEM)],
+            out_specs=(margin_spec, regress_spec),
+        )(margin, raw, head_bias)
 
     in_specs = (P(("grp", "lon"), None, None, None), P(), P(), P(), P())
     out_specs = (P(("grp", "lon"), None, None), P(("grp", "lon"), None, None, None))

time: 44.1 us -> 42.4 us (0.961)
  local copies, waits for them, and re-layouts: 3.73 us -> 0 us
  Pallas kernels: 39.5 us -> 41.6 us
    unnamed x2 -> x0, local copies, waits for them, and re-layouts: 3.73 us -> none
    pallas_call x0 -> x1, Pallas kernels: none -> 2.09 us  [shards(): pl.pallas_call(deliver, grid=(2,), out_shape=(jax.ShapeDtypeStruct(margin...]
where the time goes in v3:
time: 42.4 us; the launch traced here: 42.2 us
  Pallas kernels  41.6 us (98%)
  between operations  0.64 us (2%)
    pallas_call x1, Pallas kernels, shards(): pl.pallas_call(lambda *refs: kernel(n, *refs), out_shape=(jax.ShapeDtypeS...  39.5 us
    pallas_call x1, Pallas kernels, shards(): pl.pallas_call(deliver, grid=(2,), out_shape=(jax.ShapeDtypeStruct(margin...  2.09 us

profile of v3, /device:TPU:0, one launch (start us, length us, event | category | flops | bytes accessed | tf_op | source)
XLA Modules:
  0.0 42.2 jit_solution(14356980587987022737)
XLA Ops:
  0.6 39.5 %shard_map.68 = (f32[1,16,4096]{2,1,0:T(8,128)}, f32[1,3,16,4096]{3,2,1,0:T(8,128)}) custom-call(bf16[1,16,4096,128]{3,2,1,0:T(8,128)(2,1)} %refs_0_.1, bf16[3,3,64,128]{3,2,1,0:T(8,128)(2,1)} %bitcast.3, f32[1,64]{1,0:T(1,128)} %bitcast.5, bf16[4,64]{1,0:T(4,128)(2,1)} %bitcast.4, f32[4]{0:T(128)} %hb_ref.1), custom_call_target="tpu_custom_call" | custom-call | flops 9663676416 | bytes 16777216 | tf_op jit(solution)/shard_map/pallas_call | solution.py:346
  40.1 2.1 %shard_map.69 = (f32[1,16,4096]{2,1,0:T(8,128)}, f32[1,3,16,4096]{3,2,1,0:T(8,128)}) custom-call(f32[1,16,4096]{2,1,0:T(8,128)} %get-tuple-element.4.margin_in, f32[1,3,16,4096]{3,2,1,0:T(8,128)} %get-tuple-element.5.raw_in, f32[4]{0:T(128)} %hb_ref.1), custom_call_target="tpu_custom_call" | custom-call | tf_op jit(solution)/shard_map/pallas_call | solution.py:387
